TPU v7x, 512 devices: a whole 4x4x16 slice. The times are simulated.
512 devices in a mesh: group: 64 (over z, x), local: 8 (over y, core).
Axes of the slice: x: 4, y: 4, z: 16, core: 2. Of those that a mesh axis runs over, the one named last changes fastest.
Arguments:
- layer_input: bfloat16 [8192, 3584], P('group', 'local'), may hold values from -6 to 6
- out_grad: bfloat16 [8192, 3584], P('group', 'local'), may hold values from -6 to 6
- expert_ids: int32 [8192, 2], P('group'), may hold values from 0 to 63, all different within a row; in each aligned block of 128 rows (0 to 127, 128 to 255, ...) at most 8 rows name the same one
- gate_probs: float32 [8192, 2], P('group'), may hold values from 0.05 to 1
- w_gate: bfloat16 [64, 3584, 1024], P('group', None, 'local'), may hold values from -0.09375 to 0.09375
- w_up: bfloat16 [64, 3584, 1024], P('group', None, 'local'), may hold values from -0.09375 to 0.09375
- w_down: bfloat16 [64, 1024, 3584], P('group', 'local'), may hold values from -0.1875 to 0.1875
Outputs:
- input_grad: bfloat16 [8192, 3584], P('group', 'local')
Inputs may be any that keep to these rules, and one draw needn't show every extreme that they name: `expert_ids`: each token names 2 different experts. Among the 128 tokens held by one index of group, at most 8 name any one expert, a bound that some block reaches of them.
All inputs are finite; a program needn't handle non-finite values.
Results may differ from a plain program's by a relative error of at most 0.019.
Values may be sent and summed in bfloat16 or wider, within the bound.
No kernel may reach another device: no remote copies, remote signals or barrier semaphores. Data moves between devices by JAX's collectives and lax.ppermute only.
A program may use at most 64 MiB of HBM per device.

v0:
```python
import jax
import jax.numpy as jnp
from jax import lax
from jax.sharding import Mesh, PartitionSpec as P

N_Z, N_X, N_Y, N_C = (16, 4, 4, 2)
GROUP = ("z", "x")
LOCAL = ("y", "c")
SLOTS = 4


def dot(left, right, left_dim, right_dim):
    return lax.dot_general(
        left, right, (((left_dim,), (right_dim,)), ((), ())), preferred_element_type=jnp.float32
    )


def shift(value, axis, step, size):
    return lax.ppermute(value, axis, [(i, (i + step) % size) for i in range(size)])


def shards(layer_input, out_grad, expert_ids, gate_probs, w_gate, w_up, w_down):
    bf16 = jnp.bfloat16
    groups = N_Z * N_X
    tokens, width = layer_input.shape
    rows = groups * SLOTS
    chip = N_C * width
    core = lax.axis_index("c")
    here = lax.axis_index("y")
    own = jnp.stack([layer_input.T, out_grad.T])
    both = lax.all_gather(own, "c", axis=1, tiled=True).reshape(2 * chip, tokens)
    first, second = (expert_ids[:, 0], expert_ids[:, 1])
    position = jnp.arange(tokens, dtype=jnp.int32)
    before = position[None, :] < position[:, None]

    def rank(ids):
        same = (ids[:, None] == first[None, :]) | (ids[:, None] == second[None, :])
        return jnp.sum((same & before).astype(jnp.int32), axis=1)

    def slot_of(ids):
        place = rank(ids) - SLOTS * core
        return jnp.where((place >= 0) & (place < SLOTS), ids * SLOTS + place, -1)

    slot_ids = jnp.arange(rows, dtype=jnp.int32)
    hit_first = slot_of(first)[None, :] == slot_ids[:, None]
    hit_second = slot_of(second)[None, :] == slot_ids[:, None]
    select = (hit_first | hit_second).astype(bf16)
    weight = jnp.where(hit_first, gate_probs[:, 0][None, :], 0.0) + jnp.where(
        hit_second, gate_probs[:, 1][None, :], 0.0
    )
    weight_high = weight.astype(bf16)
    weight_low = (weight - weight_high.astype(jnp.float32)).astype(bf16)
    weights = jnp.concatenate([weight_high, weight_low], axis=1)
    send = dot(select, both, 1, 1).astype(bf16).reshape(groups, SLOTS, 2 * chip)
    send, w_gate, w_up, w_down = lax.optimization_barrier((send, w_gate, w_up, w_down))
    recv = lax.all_to_all(send, GROUP, split_axis=0, concat_axis=0, tiled=True)
    mats = jnp.stack([w_gate[0], w_up[0], w_down[0].T])

    def part(step):
        return lax.dynamic_slice_in_dim(mats, chip * ((here + step) % N_Y), chip, axis=1)

    blocks = jnp.stack([part(0)] + [shift(part(d), "y", d, N_Y) for d in range(1, N_Y)])
    other = shift(blocks, "c", 1, N_C)
    full = [jnp.concatenate([blocks[d], other[d]], axis=2) for d in range(N_Y)]
    recv = recv.reshape(rows, 2 * chip)
    rows_in, rows_grad = (recv[:, :chip], recv[:, chip:])

    def partial(d):
        return jnp.stack(
            [
                dot(rows_in, full[d][0], 1, 0),
                dot(rows_in, full[d][1], 1, 0),
                dot(rows_grad, full[d][2], 1, 0),
            ]
        )

    sums = partial(0)
    for d in range(1, N_Y):
        sums = sums + shift(partial(d).astype(bf16), "y", -d, N_Y).astype(jnp.float32)
    gate_act, up_act, hidden_grad = (sums[0], sums[1], sums[2])
    sigmoid_gate = jax.nn.sigmoid(gate_act)
    gate_grad = hidden_grad * up_act * sigmoid_gate * (1.0 + gate_act * (1.0 - sigmoid_gate))
    up_grad = hidden_grad * gate_act * sigmoid_gate
    grads = jnp.stack([gate_grad.astype(bf16), up_grad.astype(bf16)])
    back = jnp.zeros((rows, chip), jnp.float32)
    for d in range(N_Y):
        theirs = shift(grads, "y", d, N_Y) if d else grads
        back = back + dot(theirs[0], full[d][0], 1, 1) + dot(theirs[1], full[d][1], 1, 1)
    returned = lax.all_to_all(
        back.astype(bf16).reshape(groups, SLOTS, chip),
        GROUP,
        split_axis=0,
        concat_axis=0,
        tiled=True,
    ).reshape(rows, chip)
    mixed = dot(returned, weights, 0, 0)
    mixed = (mixed[:, :tokens] + mixed[:, tokens:]).reshape(N_C, width, tokens)
    mine = lax.dynamic_index_in_dim(mixed, core, 0, keepdims=False)
    sibling = lax.dynamic_index_in_dim(mixed, 1 - core, 0, keepdims=False)
    result = mine + shift(sibling, "c", 1, N_C)
    return result.astype(bf16).T


def solution(mesh):
    split = Mesh(mesh.devices.reshape(N_Z, N_X, N_Y, N_C), GROUP + LOCAL)
    placed = (
        P(GROUP, LOCAL),
        P(GROUP, LOCAL),
        P(GROUP, None),
        P(GROUP, None),
        P(GROUP, None, LOCAL),
        P(GROUP, None, LOCAL),
        P(GROUP, LOCAL, None),
    )
    return jax.shard_map(
        shards, mesh=split, in_specs=placed, out_specs=P(GROUP, LOCAL), check_vma=False
    )
```

profile of v0, /device:TPU:1, one launch (start us, length us, event | category | flops | bytes accessed | tf_op | source)
XLA Modules:
  0.0 182.8 jit_solution(13308187228344065510)
XLA Ops:
  1.7 8.6 %all_gather.3 = bf16[2,896,128]{2,1,0:T(8,128)(2,1)S(1)} all-gather(bf16[2,448,128]{2,1,0:T(8,128)(2,1)S(1)} %pad_maximum_fusion.10), channel_id=1, replica_groups=mesh['z'=16,'x'=4,'y'=4,'c'=2] {'c'}, dimensions={1}, use_global_device_ids=true | all-gather | bytes 688128 | tf_op jit(solution)/shard_map/all_gather | solution.py:31
  17.6 1.9 %collective-permute-start = (bf16[3,896,128]{1,2,0:T(8,128)(2,1)}, bf16[3,896,128]{1,2,0:T(8,128)(2,1)S(1)}, u32[]{:S(2)}, u32[]{:S(2)}) collective-permute-start(bf16[3,896,128]{1,2,0:T(8,128)(2,1)} %get-tuple-element.22), channel_id=1, source_target_pairs={{0,2},{2,4},{4,6},{6,0},{1,3},{3,5},{5,7},{7,1},{8,10},{10,12},{12... | collective-permute-start | bytes 2064392 | tf_op jit(solution)/shard_map/ppermute | solution.py:19
  19.5 1.9 %collective-permute-start.1 = (bf16[3,896,128]{1,2,0:T(8,128)(2,1)}, bf16[3,896,128]{1,2,0:T(8,128)(2,1)S(1)}, u32[]{:S(2)}, u32[]{:S(2)}) collective-permute-start(bf16[3,896,128]{1,2,0:T(8,128)(2,1)} %get-tuple-element.21), channel_id=1, source_target_pairs={{0,4},{2,6},{4,0},{6,2},{1,5},{3,7},{5,1},{7,3},{8,12},{10,14},{12... | collective-permute-start | bytes 2064392 | tf_op jit(solution)/shard_map/ppermute | solution.py:19
  21.4 4.6 %collective-permute-start.2 = (bf16[3,896,128]{1,2,0:T(8,128)(2,1)S(1)}, bf16[3,896,128]{1,2,0:T(8,128)(2,1)S(1)}, u32[]{:S(2)}, u32[]{:S(2)}) collective-permute-start(bf16[3,896,128]{1,2,0:T(8,128)(2,1)S(1)} %get-tuple-element.20), channel_id=1, source_target_pairs={{0,6},{2,0},{4,2},{6,4},{1,7},{3,1},{5,3},{7,5},{8,14},{10,8},{12,... | collective-permute-start | bytes 2064392 | tf_op jit(solution)/shard_map/ppermute | solution.py:19
  26.0 15.4 %all-to-all-start = ((bf16[64,4,1792]{2,1,0:T(4,128)(2,1)}), bf16[64,4,1792]{2,1,0:T(4,128)(2,1)}, u32[]{:S(2)}, u32[]{:S(2)}) async-start(bf16[64,4,1792]{2,1,0:T(4,128)(2,1)} %reshape.51), calls=%async_computation | async-start | bytes 1835008 | tf_op jit(solution)/shard_map/all_to_all | solution.py:56
  41.4 10.9 %collective-permute-done = bf16[3,896,128]{1,2,0:T(8,128)(2,1)S(1)} collective-permute-done((bf16[3,896,128]{1,2,0:T(8,128)(2,1)}, bf16[3,896,128]{1,2,0:T(8,128)(2,1)S(1)}, u32[]{:S(2)}, u32[]{:S(2)}) %collective-permute-start) | collective-permute-done | bytes 688160 | tf_op jit(solution)/shard_map/ppermute | solution.py:19
  52.4 2.2 %collective-permute-done.2 = bf16[3,896,128]{1,2,0:T(8,128)(2,1)S(1)} collective-permute-done((bf16[3,896,128]{1,2,0:T(8,128)(2,1)S(1)}, bf16[3,896,128]{1,2,0:T(8,128)(2,1)S(1)}, u32[]{:S(2)}, u32[]{:S(2)}) %collective-permute-start.2) | collective-permute-done | bytes 688160 | tf_op jit(solution)/shard_map/ppermute | solution.py:19
  55.4 3.3 %collective-permute-start.3 = (bf16[4,3,896,128]{2,3,1,0:T(8,128)(2,1)S(1)}, bf16[4,3,896,128]{2,3,1,0:T(8,128)(2,1)S(1)}, u32[]{:S(2)}, u32[]{:S(2)}) collective-permute-start(bf16[4,3,896,128]{2,3,1,0:T(8,128)(2,1)S(1)} %pad_maximum_fusion.1), channel_id=1, source_target_pairs={{0,1},{1,0},{2,3},{3,2},{4,5},{5,4},{6,7},{7,6},{8,9},{9,8},{10,11... | collective-permute-start | bytes 8257544 | tf_op jit(solution)/shard_map/ppermute | solution.py:19
  58.7 4.7 %collective-permute-done.3 = bf16[4,3,896,128]{2,3,1,0:T(8,128)(2,1)S(1)} collective-permute-done((bf16[4,3,896,128]{2,3,1,0:T(8,128)(2,1)S(1)}, bf16[4,3,896,128]{2,3,1,0:T(8,128)(2,1)S(1)}, u32[]{:S(2)}, u32[]{:S(2)}) %collective-permute-start.3) | collective-permute-done | bytes 2752544 | tf_op jit(solution)/shard_map/ppermute | solution.py:19
  64.8 22.3 %all-to-all-done = bf16[64,4,1792]{2,1,0:T(4,128)(2,1)} async-done(((bf16[64,4,1792]{2,1,0:T(4,128)(2,1)}), bf16[64,4,1792]{2,1,0:T(4,128)(2,1)}, u32[]{:S(2)}, u32[]{:S(2)}) %all-to-all-start) | async-done | bytes 917536 | tf_op jit(solution)/shard_map/all_to_all | solution.py:56
  87.2 1.6 reshape.52
  91.0 2.0 %collective-permute-start.4 = (bf16[3,256,256]{2,1,0:T(8,128)(2,1)S(1)}, bf16[3,256,256]{2,1,0:T(8,128)(2,1)S(1)}, u32[]{:S(2)}, u32[]{:S(2)}) collective-permute-start(bf16[3,256,256]{2,1,0:T(8,128)(2,1)S(1)} %pad_maximum_fusion.6), channel_id=1, source_target_pairs={{0,6},{2,0},{4,2},{6,4},{1,7},{3,1},{5,3},{7,5},{8,14},{10,8},{12,... | collective-permute-start | bytes 1179656 | tf_op jit(solution)/shard_map/ppermute | solution.py:19
  94.0 4.0 %collective-permute-start.5 = (bf16[3,256,256]{2,1,0:T(8,128)(2,1)S(1)}, bf16[3,256,256]{2,1,0:T(8,128)(2,1)S(1)}, u32[]{:S(2)}, u32[]{:S(2)}) collective-permute-start(bf16[3,256,256]{2,1,0:T(8,128)(2,1)S(1)} %pad_maximum_fusion.7), channel_id=1, source_target_pairs={{0,4},{2,6},{4,0},{6,2},{1,5},{3,7},{5,1},{7,3},{8,12},{10,14},{12... | collective-permute-start | bytes 1179656 | tf_op jit(solution)/shard_map/ppermute | solution.py:19
  99.2 1.9 %collective-permute-start.6 = (bf16[3,256,256]{2,1,0:T(8,128)(2,1)S(1)}, bf16[3,256,256]{2,1,0:T(8,128)(2,1)S(1)}, u32[]{:S(2)}, u32[]{:S(2)}) collective-permute-start(bf16[3,256,256]{2,1,0:T(8,128)(2,1)S(1)} %pad_maximum_fusion.8), channel_id=1, source_target_pairs={{0,2},{2,4},{4,6},{6,0},{1,3},{3,5},{5,7},{7,1},{8,10},{10,12},{12... | collective-permute-start | bytes 1179656 | tf_op jit(solution)/shard_map/ppermute | solution.py:19
  102.1 1.9 %collective-permute-done.5 = bf16[3,256,256]{2,1,0:T(8,128)(2,1)S(1)} collective-permute-done((bf16[3,256,256]{2,1,0:T(8,128)(2,1)S(1)}, bf16[3,256,256]{2,1,0:T(8,128)(2,1)S(1)}, u32[]{:S(2)}, u32[]{:S(2)}) %collective-permute-start.5) | collective-permute-done | bytes 393248 | tf_op jit(solution)/shard_map/ppermute | solution.py:19
  104.0 10.3 %collective-permute-done.6 = bf16[3,256,256]{2,1,0:T(8,128)(2,1)S(1)} collective-permute-done((bf16[3,256,256]{2,1,0:T(8,128)(2,1)S(1)}, bf16[3,256,256]{2,1,0:T(8,128)(2,1)S(1)}, u32[]{:S(2)}, u32[]{:S(2)}) %collective-permute-start.6) | collective-permute-done | bytes 393248 | tf_op jit(solution)/shard_map/ppermute | solution.py:19
  115.0 1.9 %collective-permute-start.7 = (bf16[2,256,256]{2,1,0:T(8,128)(2,1)S(1)}, bf16[2,256,256]{2,1,0:T(8,128)(2,1)S(1)}, u32[]{:S(2)}, u32[]{:S(2)}) collective-permute-start(bf16[2,256,256]{2,1,0:T(8,128)(2,1)S(1)} %pad_maximum_fusion.9), channel_id=1, source_target_pairs={{0,2},{2,4},{4,6},{6,0},{1,3},{3,5},{5,7},{7,1},{8,10},{10,12},{12... | collective-permute-start | bytes 786440 | tf_op jit(solution)/shard_map/ppermute | solution.py:19
  116.9 4.0 %collective-permute-start.8 = (bf16[2,256,256]{2,1,0:T(8,128)(2,1)S(1)}, bf16[2,256,256]{2,1,0:T(8,128)(2,1)S(1)}, u32[]{:S(2)}, u32[]{:S(2)}) collective-permute-start(bf16[2,256,256]{2,1,0:T(8,128)(2,1)S(1)} %pad_maximum_fusion.9), channel_id=1, source_target_pairs={{0,4},{2,6},{4,0},{6,2},{1,5},{3,7},{5,1},{7,3},{8,12},{10,14},{12... | collective-permute-start | bytes 786440 | tf_op jit(solution)/shard_map/ppermute | solution.py:19
  120.9 4.0 %collective-permute-start.9 = (bf16[2,256,256]{2,1,0:T(8,128)(2,1)S(1)}, bf16[2,256,256]{2,1,0:T(8,128)(2,1)S(1)}, u32[]{:S(2)}, u32[]{:S(2)}) collective-permute-start(bf16[2,256,256]{2,1,0:T(8,128)(2,1)S(1)} %pad_maximum_fusion.9), channel_id=1, source_target_pairs={{0,6},{2,0},{4,2},{6,4},{1,7},{3,1},{5,3},{7,5},{8,14},{10,8},{12,... | collective-permute-start | bytes 786440 | tf_op jit(solution)/shard_map/ppermute | solution.py:19
  125.2 2.4 %collective-permute-done.8 = bf16[2,256,256]{2,1,0:T(8,128)(2,1)S(1)} collective-permute-done((bf16[2,256,256]{2,1,0:T(8,128)(2,1)S(1)}, bf16[2,256,256]{2,1,0:T(8,128)(2,1)S(1)}, u32[]{:S(2)}, u32[]{:S(2)}) %collective-permute-start.8) | collective-permute-done | bytes 262176 | tf_op jit(solution)/shard_map/ppermute | solution.py:19
  128.2 1.9 %collective-permute-done.9 = bf16[2,256,256]{2,1,0:T(8,128)(2,1)S(1)} collective-permute-done((bf16[2,256,256]{2,1,0:T(8,128)(2,1)S(1)}, bf16[2,256,256]{2,1,0:T(8,128)(2,1)S(1)}, u32[]{:S(2)}, u32[]{:S(2)}) %collective-permute-start.9) | collective-permute-done | bytes 262176 | tf_op jit(solution)/shard_map/ppermute | solution.py:19
  132.4 14.8 %all-to-all-start.1 = ((bf16[64,4,896]{2,1,0:T(4,128)(2,1)}), bf16[64,4,896]{2,1,0:T(4,128)(2,1)S(1)}, u32[]{:S(2)}, u32[]{:S(2)}) async-start(bf16[64,4,896]{2,1,0:T(4,128)(2,1)} %reshape.53), calls=%async_computation.1 | async-start | bytes 917504 | tf_op jit(solution)/shard_map/all_to_all | solution.py:89
  147.3 26.4 %all-to-all-done.1 = bf16[64,4,896]{2,1,0:T(4,128)(2,1)S(1)} async-done(((bf16[64,4,896]{2,1,0:T(4,128)(2,1)}), bf16[64,4,896]{2,1,0:T(4,128)(2,1)S(1)}, u32[]{:S(2)}, u32[]{:S(2)}) %all-to-all-start.1) | async-done | bytes 458784 | tf_op jit(solution)/shard_map/all_to_all | solution.py:89
  174.2 6.8 %collective-permute-start.10 = (f32[448,128]{1,0:T(8,128)S(1)}, f32[448,128]{1,0:T(8,128)S(1)}, u32[]{:S(2)}, u32[]{:S(2)}) collective-permute-start(f32[448,128]{1,0:T(8,128)S(1)} %dynamic-slice_bitcast_fusion), channel_id=1, source_target_pairs={{0,1},{1,0},{2,3},{3,2},{4,5},{5,4},{6,7},{7,6},{8,9},{9,8},{10,11... | collective-permute-start | bytes 688136 | tf_op jit(solution)/shard_map/ppermute | solution.py:19
  (70 shorter events, 22.3 us)
Async XLA Ops:
  11.3 1.6 copy-start.7
  12.9 1.2 copy-start.8
  17.6 34.8 %collective-permute-start = (bf16[3,896,128]{1,2,0:T(8,128)(2,1)}, bf16[3,896,128]{1,2,0:T(8,128)(2,1)S(1)}, u32[]{:S(2)}, u32[]{:S(2)}) collective-permute-start(bf16[3,896,128]{1,2,0:T(8,128)(2,1)} %get-tuple-element.22), channel_id=1, source_target_pairs={{0,2},{2,4},{4,6},{6,0},{1,3},{3,5},{5,7},{7,1},{8,10},{10,12},{12... | collective-permute-start | bytes 2064392 | tf_op jit(solution)/shard_map/ppermute | solution.py:19
  19.5 32.9 %collective-permute-start.1 = (bf16[3,896,128]{1,2,0:T(8,128)(2,1)}, bf16[3,896,128]{1,2,0:T(8,128)(2,1)S(1)}, u32[]{:S(2)}, u32[]{:S(2)}) collective-permute-start(bf16[3,896,128]{1,2,0:T(8,128)(2,1)} %get-tuple-element.21), channel_id=1, source_target_pairs={{0,4},{2,6},{4,0},{6,2},{1,5},{3,7},{5,1},{7,3},{8,12},{10,14},{12... | collective-permute-start | bytes 2064392 | tf_op jit(solution)/shard_map/ppermute | solution.py:19
  21.4 33.2 %collective-permute-start.2 = (bf16[3,896,128]{1,2,0:T(8,128)(2,1)S(1)}, bf16[3,896,128]{1,2,0:T(8,128)(2,1)S(1)}, u32[]{:S(2)}, u32[]{:S(2)}) collective-permute-start(bf16[3,896,128]{1,2,0:T(8,128)(2,1)S(1)} %get-tuple-element.20), channel_id=1, source_target_pairs={{0,6},{2,0},{4,2},{6,4},{1,7},{3,1},{5,3},{7,5},{8,14},{10,8},{12,... | collective-permute-start | bytes 2064392 | tf_op jit(solution)/shard_map/ppermute | solution.py:19
  26.0 61.2 %all-to-all-start = ((bf16[64,4,1792]{2,1,0:T(4,128)(2,1)}), bf16[64,4,1792]{2,1,0:T(4,128)(2,1)}, u32[]{:S(2)}, u32[]{:S(2)}) async-start(bf16[64,4,1792]{2,1,0:T(4,128)(2,1)} %reshape.51), calls=%async_computation | async-start | bytes 1835008 | tf_op jit(solution)/shard_map/all_to_all | solution.py:56
  52.4 2.7 %copy-start.3 = (bf16[3,896,128]{1,2,0:T(8,128)(2,1)}, bf16[3,896,128]{1,2,0:T(8,128)(2,1)S(1)}, u32[]{:S(2)}) copy-start(bf16[3,896,128]{1,2,0:T(8,128)(2,1)S(1)} %collective-permute-done.1) | copy-start | bytes 2064388
  54.6 0.8 copy-start.1
  55.4 8.0 %collective-permute-start.3 = (bf16[4,3,896,128]{2,3,1,0:T(8,128)(2,1)S(1)}, bf16[4,3,896,128]{2,3,1,0:T(8,128)(2,1)S(1)}, u32[]{:S(2)}, u32[]{:S(2)}) collective-permute-start(bf16[4,3,896,128]{2,3,1,0:T(8,128)(2,1)S(1)} %pad_maximum_fusion.1), channel_id=1, source_target_pairs={{0,1},{1,0},{2,3},{3,2},{4,5},{5,4},{6,7},{7,6},{8,9},{9,8},{10,11... | collective-permute-start | bytes 8257544 | tf_op jit(solution)/shard_map/ppermute | solution.py:19
  88.8 1.4 copy-start
  90.5 2.4 %copy-start.4 = (bf16[3,896,128]{1,2,0:T(8,128)(2,1)S(1)}, bf16[3,896,128]{1,2,0:T(8,128)(2,1)}, u32[]{:S(2)}) copy-start(bf16[3,896,128]{1,2,0:T(8,128)(2,1)} %copy-done.3) | copy-start | bytes 2064388
  90.5 2.4 %copy-start.6 = (bf16[3,896,128]{1,2,0:T(8,128)(2,1)S(1)}, bf16[3,896,128]{1,2,0:T(8,128)(2,1)}, u32[]{:S(2)}) copy-start(bf16[3,896,128]{1,2,0:T(8,128)(2,1)} %get-tuple-element.17) | copy-start | bytes 2064388
  91.0 11.1 %collective-permute-start.4 = (bf16[3,256,256]{2,1,0:T(8,128)(2,1)S(1)}, bf16[3,256,256]{2,1,0:T(8,128)(2,1)S(1)}, u32[]{:S(2)}, u32[]{:S(2)}) collective-permute-start(bf16[3,256,256]{2,1,0:T(8,128)(2,1)S(1)} %pad_maximum_fusion.6), channel_id=1, source_target_pairs={{0,6},{2,0},{4,2},{6,4},{1,7},{3,1},{5,3},{7,5},{8,14},{10,8},{12,... | collective-permute-start | bytes 1179656 | tf_op jit(solution)/shard_map/ppermute | solution.py:19
  93.6 4.5 %copy-start.2 = (bf16[3,896,128]{1,2,0:T(8,128)(2,1)S(1)}, bf16[3,896,128]{1,2,0:T(8,128)(2,1)}, u32[]{:S(2)}) copy-start(bf16[3,896,128]{1,2,0:T(8,128)(2,1)} %copy-done.1) | copy-start | bytes 2064388
  93.6 4.5 %copy-start.5 = (bf16[3,896,128]{1,2,0:T(8,128)(2,1)S(1)}, bf16[3,896,128]{1,2,0:T(8,128)(2,1)}, u32[]{:S(2)}) copy-start(bf16[3,896,128]{1,2,0:T(8,128)(2,1)} %get-tuple-element.16) | copy-start | bytes 2064388
  94.0 10.0 %collective-permute-start.5 = (bf16[3,256,256]{2,1,0:T(8,128)(2,1)S(1)}, bf16[3,256,256]{2,1,0:T(8,128)(2,1)S(1)}, u32[]{:S(2)}, u32[]{:S(2)}) collective-permute-start(bf16[3,256,256]{2,1,0:T(8,128)(2,1)S(1)} %pad_maximum_fusion.7), channel_id=1, source_target_pairs={{0,4},{2,6},{4,0},{6,2},{1,5},{3,7},{5,1},{7,3},{8,12},{10,14},{12... | collective-permute-start | bytes 1179656 | tf_op jit(solution)/shard_map/ppermute | solution.py:19
  99.2 15.2 %collective-permute-start.6 = (bf16[3,256,256]{2,1,0:T(8,128)(2,1)S(1)}, bf16[3,256,256]{2,1,0:T(8,128)(2,1)S(1)}, u32[]{:S(2)}, u32[]{:S(2)}) collective-permute-start(bf16[3,256,256]{2,1,0:T(8,128)(2,1)S(1)} %pad_maximum_fusion.8), channel_id=1, source_target_pairs={{0,2},{2,4},{4,6},{6,0},{1,3},{3,5},{5,7},{7,1},{8,10},{10,12},{12... | collective-permute-start | bytes 1179656 | tf_op jit(solution)/shard_map/ppermute | solution.py:19
  115.0 15.7 %collective-permute-start.7 = (bf16[2,256,256]{2,1,0:T(8,128)(2,1)S(1)}, bf16[2,256,256]{2,1,0:T(8,128)(2,1)S(1)}, u32[]{:S(2)}, u32[]{:S(2)}) collective-permute-start(bf16[2,256,256]{2,1,0:T(8,128)(2,1)S(1)} %pad_maximum_fusion.9), channel_id=1, source_target_pairs={{0,2},{2,4},{4,6},{6,0},{1,3},{3,5},{5,7},{7,1},{8,10},{10,12},{12... | collective-permute-start | bytes 786440 | tf_op jit(solution)/shard_map/ppermute | solution.py:19
  116.9 10.6 %collective-permute-start.8 = (bf16[2,256,256]{2,1,0:T(8,128)(2,1)S(1)}, bf16[2,256,256]{2,1,0:T(8,128)(2,1)S(1)}, u32[]{:S(2)}, u32[]{:S(2)}) collective-permute-start(bf16[2,256,256]{2,1,0:T(8,128)(2,1)S(1)} %pad_maximum_fusion.9), channel_id=1, source_target_pairs={{0,4},{2,6},{4,0},{6,2},{1,5},{3,7},{5,1},{7,3},{8,12},{10,14},{12... | collective-permute-start | bytes 786440 | tf_op jit(solution)/shard_map/ppermute | solution.py:19
  120.9 9.2 %collective-permute-start.9 = (bf16[2,256,256]{2,1,0:T(8,128)(2,1)S(1)}, bf16[2,256,256]{2,1,0:T(8,128)(2,1)S(1)}, u32[]{:S(2)}, u32[]{:S(2)}) collective-permute-start(bf16[2,256,256]{2,1,0:T(8,128)(2,1)S(1)} %pad_maximum_fusion.9), channel_id=1, source_target_pairs={{0,6},{2,0},{4,2},{6,4},{1,7},{3,1},{5,3},{7,5},{8,14},{10,8},{12,... | collective-permute-start | bytes 786440 | tf_op jit(solution)/shard_map/ppermute | solution.py:19
  131.5 15.7 %copy-start.9 = (f32[128,2]{0,1:T(2,128)S(1)}, f32[128,2]{0,1:T(2,128)}, u32[]{:S(2)}) copy-start(f32[128,2]{0,1:T(2,128)} %param.10) | copy-start | bytes 3076
  132.4 41.3 %all-to-all-start.1 = ((bf16[64,4,896]{2,1,0:T(4,128)(2,1)}), bf16[64,4,896]{2,1,0:T(4,128)(2,1)S(1)}, u32[]{:S(2)}, u32[]{:S(2)}) async-start(bf16[64,4,896]{2,1,0:T(4,128)(2,1)} %reshape.53), calls=%async_computation.1 | async-start | bytes 917504 | tf_op jit(solution)/shard_map/all_to_all | solution.py:89
  174.2 7.9 %collective-permute-start.10 = (f32[448,128]{1,0:T(8,128)S(1)}, f32[448,128]{1,0:T(8,128)S(1)}, u32[]{:S(2)}, u32[]{:S(2)}) collective-permute-start(f32[448,128]{1,0:T(8,128)S(1)} %dynamic-slice_bitcast_fusion), channel_id=1, source_target_pairs={{0,1},{1,0},{2,3},{3,2},{4,5},{5,4},{6,7},{7,6},{8,9},{9,8},{10,11... | collective-permute-start | bytes 688136 | tf_op jit(solution)/shard_map/ppermute | solution.py:19
where the time goes:
time: 184 us; the launch traced here: 183 us
  waiting for transfers between devices  84.2 us (46%)
  starting transfers between devices  66.6 us (36%)
  local copies, waits for them, and re-layouts  9.55 us (5%)
  blocking collectives  8.64 us (5%)
  matrix products  8.25 us (4%)
  other arithmetic  5.06 us (3%)
    ppermute x11, starting transfers between devices, shift(): lax.ppermute(value, axis, [(i, (i + step) % size) for i in range(size)])  36.3 us
    ppermute x11, waiting for transfers between devices, shift(): lax.ppermute(value, axis, [(i, (i + step) % size) for i in range(size)])  35.5 us
    all_to_all x1, waiting for transfers between devices, shards(): lax.all_to_all(back.astype(bf16).reshape(groups, SLOTS, chip), GROUP, spl...  26.4 us
    all_to_all x1, waiting for transfers between devices, shards(): recv = lax.all_to_all(send, GROUP, split_axis=0, concat_axis=0, tiled=True)  22.3 us
    all_to_all x1, starting transfers between devices, shards(): recv = lax.all_to_all(send, GROUP, split_axis=0, concat_axis=0, tiled=True)  15.4 us
    all_to_all x1, starting transfers between devices, shards(): lax.all_to_all(back.astype(bf16).reshape(groups, SLOTS, chip), GROUP, spl...  14.8 us
    all_gather x1, blocking collectives, shards(): lax.all_gather(own, 'c', axis=1, tiled=True).reshape(2 * chip, tokens)  8.64 us
    dot_general x22, matrix products, dot(): lax.dot_general(left, right, (((left_dim,), (right_dim,)), ((), ())), pre...  8.25 us
  transfers between devices with their start and end apart: 13, of which 10 were waited for; matrix products, arithmetic and copies ran while one was open for 4% of the time, Pallas kernels for 0%

commit v1 on v0

--- a/solution.py
+++ b/solution.py
@@ -28,7 +28,9 @@
     core = lax.axis_index("c")
     here = lax.axis_index("y")
     own = jnp.stack([layer_input.T, out_grad.T])
-    both = lax.all_gather(own, "c", axis=1, tiled=True).reshape(2 * chip, tokens)
+    both = jnp.concatenate(
+        lax.all_to_all(jnp.stack([own] * lax.axis_size("c")), "c", 0, 0), axis=1
+    ).reshape(2 * chip, tokens)
     first, second = (expert_ids[:, 0], expert_ids[:, 1])
     position = jnp.arange(tokens, dtype=jnp.int32)
     before = position[None, :] < position[:, None]

time: 184 us -> 186 us (1.011)
  starting transfers between devices: 66.6 us -> 76.9 us
  blocking collectives: 8.64 us -> 0 us
    all_to_all x0 -> x1, starting transfers between devices: none -> 10.3 us  [shards(): lax.all_to_all(jnp.stack([own] * lax.axis_size('c')), 'c', 0, 0)]
    all_gather x1 -> x0, blocking collectives: 8.64 us -> none  [shards(): lax.all_gather(own, 'c', axis=1, tiled=True).reshape(2 * chip, tokens)]
  transfers between devices with their start and end apart: 13 -> 14, of which waited for: 10 -> 11; matrix products, arithmetic and copies ran while one was open for 4% -> 4% of each run, Pallas kernels for 0% -> 0%
where the time goes in v1:
time: 186 us; the launch traced here: 185 us
  waiting for transfers between devices  85.3 us (46%)
  starting transfers between devices  76.9 us (41%)
  local copies, waits for them, and re-layouts  8.83 us (5%)
  matrix products  8.26 us (4%)
  other arithmetic  5.12 us (3%)
    ppermute x11, starting transfers between devices, shift(): lax.ppermute(value, axis, [(i, (i + step) % size) for i in range(size)])  36.3 us
    ppermute x11, waiting for transfers between devices, shift(): lax.ppermute(value, axis, [(i, (i + step) % size) for i in range(size)])  35.5 us
    all_to_all x1, waiting for transfers between devices, shards(): lax.all_to_all(back.astype(bf16).reshape(groups, SLOTS, chip), GROUP, spl...  26.4 us
    all_to_all x1, waiting for transfers between devices, shards(): recv = lax.all_to_all(send, GROUP, split_axis=0, concat_axis=0, tiled=True)  22.3 us
    all_to_all x1, starting transfers between devices, shards(): recv = lax.all_to_all(send, GROUP, split_axis=0, concat_axis=0, tiled=True)  15.4 us
    all_to_all x1, starting transfers between devices, shards(): lax.all_to_all(back.astype(bf16).reshape(groups, SLOTS, chip), GROUP, spl...  14.9 us
    all_to_all x1, starting transfers between devices, shards(): lax.all_to_all(jnp.stack([own] * lax.axis_size('c')), 'c', 0, 0)  10.3 us
    dot_general x22, matrix products, dot(): lax.dot_general(left, right, (((left_dim,), (right_dim,)), ((), ())), pre...  8.26 us
  transfers between devices with their start and end apart: 14, of which 11 were waited for; matrix products, arithmetic and copies ran while one was open for 4% of the time, Pallas kernels for 0%

profile of v1, /device:TPU:1, one launch (start us, length us, event | category | flops | bytes accessed | tf_op | source)
XLA Modules:
  0.0 185.0 jit_solution(15361209769939282012)
XLA Ops:
  1.8 10.3 %all-to-all-start = ((bf16[2,2,448,128]{3,2,1,0:T(8,128)(2,1)}), bf16[2,2,448,128]{3,2,1,0:T(8,128)(2,1)S(1)}, u32[]{:S(2)}, u32[]{:S(2)}) async-start(bf16[2,2,448,128]{3,2,1,0:T(8,128)(2,1)} %pad_maximum_fusion.6), calls=%async_computation | async-start | bytes 917504 | tf_op jit(solution)/shard_map/all_to_all | solution.py:32
  19.8 1.9 %collective-permute-start = (bf16[3,896,128]{1,2,0:T(8,128)(2,1)}, bf16[3,896,128]{1,2,0:T(8,128)(2,1)S(1)}, u32[]{:S(2)}, u32[]{:S(2)}) collective-permute-start(bf16[3,896,128]{1,2,0:T(8,128)(2,1)} %get-tuple-element.22), channel_id=1, source_target_pairs={{0,2},{2,4},{4,6},{6,0},{1,3},{3,5},{5,7},{7,1},{8,10},{10,12},{12... | collective-permute-start | bytes 2064392 | tf_op jit(solution)/shard_map/ppermute | solution.py:19
  21.7 1.9 %collective-permute-start.1 = (bf16[3,896,128]{1,2,0:T(8,128)(2,1)}, bf16[3,896,128]{1,2,0:T(8,128)(2,1)S(1)}, u32[]{:S(2)}, u32[]{:S(2)}) collective-permute-start(bf16[3,896,128]{1,2,0:T(8,128)(2,1)} %get-tuple-element.21), channel_id=1, source_target_pairs={{0,4},{2,6},{4,0},{6,2},{1,5},{3,7},{5,1},{7,3},{8,12},{10,14},{12... | collective-permute-start | bytes 2064392 | tf_op jit(solution)/shard_map/ppermute | solution.py:19
  23.6 4.6 %collective-permute-start.2 = (bf16[3,896,128]{1,2,0:T(8,128)(2,1)S(1)}, bf16[3,896,128]{1,2,0:T(8,128)(2,1)S(1)}, u32[]{:S(2)}, u32[]{:S(2)}) collective-permute-start(bf16[3,896,128]{1,2,0:T(8,128)(2,1)S(1)} %get-tuple-element.20), channel_id=1, source_target_pairs={{0,6},{2,0},{4,2},{6,4},{1,7},{3,1},{5,3},{7,5},{8,14},{10,8},{12,... | collective-permute-start | bytes 2064392 | tf_op jit(solution)/shard_map/ppermute | solution.py:19
  28.2 15.4 %all-to-all-start.1 = ((bf16[64,4,1792]{2,1,0:T(4,128)(2,1)}), bf16[64,4,1792]{2,1,0:T(4,128)(2,1)}, u32[]{:S(2)}, u32[]{:S(2)}) async-start(bf16[64,4,1792]{2,1,0:T(4,128)(2,1)} %reshape.51), calls=%async_computation.1 | async-start | bytes 1835008 | tf_op jit(solution)/shard_map/all_to_all | solution.py:58
  43.6 10.9 %collective-permute-done = bf16[3,896,128]{1,2,0:T(8,128)(2,1)S(1)} collective-permute-done((bf16[3,896,128]{1,2,0:T(8,128)(2,1)}, bf16[3,896,128]{1,2,0:T(8,128)(2,1)S(1)}, u32[]{:S(2)}, u32[]{:S(2)}) %collective-permute-start) | collective-permute-done | bytes 688160 | tf_op jit(solution)/shard_map/ppermute | solution.py:19
  54.6 2.2 %collective-permute-done.2 = bf16[3,896,128]{1,2,0:T(8,128)(2,1)S(1)} collective-permute-done((bf16[3,896,128]{1,2,0:T(8,128)(2,1)S(1)}, bf16[3,896,128]{1,2,0:T(8,128)(2,1)S(1)}, u32[]{:S(2)}, u32[]{:S(2)}) %collective-permute-start.2) | collective-permute-done | bytes 688160 | tf_op jit(solution)/shard_map/ppermute | solution.py:19
  57.6 3.3 %collective-permute-start.3 = (bf16[4,3,896,128]{2,3,1,0:T(8,128)(2,1)S(1)}, bf16[4,3,896,128]{2,3,1,0:T(8,128)(2,1)S(1)}, u32[]{:S(2)}, u32[]{:S(2)}) collective-permute-start(bf16[4,3,896,128]{2,3,1,0:T(8,128)(2,1)S(1)} %pad_maximum_fusion.1), channel_id=1, source_target_pairs={{0,1},{1,0},{2,3},{3,2},{4,5},{5,4},{6,7},{7,6},{8,9},{9,8},{10,11... | collective-permute-start | bytes 8257544 | tf_op jit(solution)/shard_map/ppermute | solution.py:19
  60.9 4.7 %collective-permute-done.3 = bf16[4,3,896,128]{2,3,1,0:T(8,128)(2,1)S(1)} collective-permute-done((bf16[4,3,896,128]{2,3,1,0:T(8,128)(2,1)S(1)}, bf16[4,3,896,128]{2,3,1,0:T(8,128)(2,1)S(1)}, u32[]{:S(2)}, u32[]{:S(2)}) %collective-permute-start.3) | collective-permute-done | bytes 2752544 | tf_op jit(solution)/shard_map/ppermute | solution.py:19
  67.0 22.3 %all-to-all-done.1 = bf16[64,4,1792]{2,1,0:T(4,128)(2,1)} async-done(((bf16[64,4,1792]{2,1,0:T(4,128)(2,1)}), bf16[64,4,1792]{2,1,0:T(4,128)(2,1)}, u32[]{:S(2)}, u32[]{:S(2)}) %all-to-all-start.1) | async-done | bytes 917536 | tf_op jit(solution)/shard_map/all_to_all | solution.py:58
  89.4 1.6 reshape.52
  93.1 1.9 %collective-permute-start.4 = (bf16[3,256,256]{2,1,0:T(8,128)(2,1)S(1)}, bf16[3,256,256]{2,1,0:T(8,128)(2,1)S(1)}, u32[]{:S(2)}, u32[]{:S(2)}) collective-permute-start(bf16[3,256,256]{2,1,0:T(8,128)(2,1)S(1)} %pad_maximum_fusion.7), channel_id=1, source_target_pairs={{0,6},{2,0},{4,2},{6,4},{1,7},{3,1},{5,3},{7,5},{8,14},{10,8},{12,... | collective-permute-start | bytes 1179656 | tf_op jit(solution)/shard_map/ppermute | solution.py:19
  96.2 4.0 %collective-permute-start.5 = (bf16[3,256,256]{2,1,0:T(8,128)(2,1)S(1)}, bf16[3,256,256]{2,1,0:T(8,128)(2,1)S(1)}, u32[]{:S(2)}, u32[]{:S(2)}) collective-permute-start(bf16[3,256,256]{2,1,0:T(8,128)(2,1)S(1)} %pad_maximum_fusion.8), channel_id=1, source_target_pairs={{0,4},{2,6},{4,0},{6,2},{1,5},{3,7},{5,1},{7,3},{8,12},{10,14},{12... | collective-permute-start | bytes 1179656 | tf_op jit(solution)/shard_map/ppermute | solution.py:19
  101.3 1.9 %collective-permute-start.6 = (bf16[3,256,256]{2,1,0:T(8,128)(2,1)S(1)}, bf16[3,256,256]{2,1,0:T(8,128)(2,1)S(1)}, u32[]{:S(2)}, u32[]{:S(2)}) collective-permute-start(bf16[3,256,256]{2,1,0:T(8,128)(2,1)S(1)} %pad_maximum_fusion.9), channel_id=1, source_target_pairs={{0,2},{2,4},{4,6},{6,0},{1,3},{3,5},{5,7},{7,1},{8,10},{10,12},{12... | collective-permute-start | bytes 1179656 | tf_op jit(solution)/shard_map/ppermute | solution.py:19
  104.3 2.0 %collective-permute-done.5 = bf16[3,256,256]{2,1,0:T(8,128)(2,1)S(1)} collective-permute-done((bf16[3,256,256]{2,1,0:T(8,128)(2,1)S(1)}, bf16[3,256,256]{2,1,0:T(8,128)(2,1)S(1)}, u32[]{:S(2)}, u32[]{:S(2)}) %collective-permute-start.5) | collective-permute-done | bytes 393248 | tf_op jit(solution)/shard_map/ppermute | solution.py:19
  106.2 10.3 %collective-permute-done.6 = bf16[3,256,256]{2,1,0:T(8,128)(2,1)S(1)} collective-permute-done((bf16[3,256,256]{2,1,0:T(8,128)(2,1)S(1)}, bf16[3,256,256]{2,1,0:T(8,128)(2,1)S(1)}, u32[]{:S(2)}, u32[]{:S(2)}) %collective-permute-start.6) | collective-permute-done | bytes 393248 | tf_op jit(solution)/shard_map/ppermute | solution.py:19
  117.2 1.9 %collective-permute-start.7 = (bf16[2,256,256]{2,1,0:T(8,128)(2,1)S(1)}, bf16[2,256,256]{2,1,0:T(8,128)(2,1)S(1)}, u32[]{:S(2)}, u32[]{:S(2)}) collective-permute-start(bf16[2,256,256]{2,1,0:T(8,128)(2,1)S(1)} %pad_maximum_fusion.10), channel_id=1, source_target_pairs={{0,2},{2,4},{4,6},{6,0},{1,3},{3,5},{5,7},{7,1},{8,10},{10,12},{12... | collective-permute-start | bytes 786440 | tf_op jit(solution)/shard_map/ppermute | solution.py:19
  119.1 4.0 %collective-permute-start.8 = (bf16[2,256,256]{2,1,0:T(8,128)(2,1)S(1)}, bf16[2,256,256]{2,1,0:T(8,128)(2,1)S(1)}, u32[]{:S(2)}, u32[]{:S(2)}) collective-permute-start(bf16[2,256,256]{2,1,0:T(8,128)(2,1)S(1)} %pad_maximum_fusion.10), channel_id=1, source_target_pairs={{0,4},{2,6},{4,0},{6,2},{1,5},{3,7},{5,1},{7,3},{8,12},{10,14},{12... | collective-permute-start | bytes 786440 | tf_op jit(solution)/shard_map/ppermute | solution.py:19
  123.1 4.0 %collective-permute-start.9 = (bf16[2,256,256]{2,1,0:T(8,128)(2,1)S(1)}, bf16[2,256,256]{2,1,0:T(8,128)(2,1)S(1)}, u32[]{:S(2)}, u32[]{:S(2)}) collective-permute-start(bf16[2,256,256]{2,1,0:T(8,128)(2,1)S(1)} %pad_maximum_fusion.10), channel_id=1, source_target_pairs={{0,6},{2,0},{4,2},{6,4},{1,7},{3,1},{5,3},{7,5},{8,14},{10,8},{12,... | collective-permute-start | bytes 786440 | tf_op jit(solution)/shard_map/ppermute | solution.py:19
  127.4 2.3 %collective-permute-done.8 = bf16[2,256,256]{2,1,0:T(8,128)(2,1)S(1)} collective-permute-done((bf16[2,256,256]{2,1,0:T(8,128)(2,1)S(1)}, bf16[2,256,256]{2,1,0:T(8,128)(2,1)S(1)}, u32[]{:S(2)}, u32[]{:S(2)}) %collective-permute-start.8) | collective-permute-done | bytes 262176 | tf_op jit(solution)/shard_map/ppermute | solution.py:19
  130.3 2.0 %collective-permute-done.9 = bf16[2,256,256]{2,1,0:T(8,128)(2,1)S(1)} collective-permute-done((bf16[2,256,256]{2,1,0:T(8,128)(2,1)S(1)}, bf16[2,256,256]{2,1,0:T(8,128)(2,1)S(1)}, u32[]{:S(2)}, u32[]{:S(2)}) %collective-permute-start.9) | collective-permute-done | bytes 262176 | tf_op jit(solution)/shard_map/ppermute | solution.py:19
  134.6 14.9 %all-to-all-start.2 = ((bf16[64,4,896]{2,1,0:T(4,128)(2,1)}), bf16[64,4,896]{2,1,0:T(4,128)(2,1)S(1)}, u32[]{:S(2)}, u32[]{:S(2)}) async-start(bf16[64,4,896]{2,1,0:T(4,128)(2,1)} %reshape.53), calls=%async_computation.2 | async-start | bytes 917504 | tf_op jit(solution)/shard_map/all_to_all | solution.py:91
  149.5 26.4 %all-to-all-done.2 = bf16[64,4,896]{2,1,0:T(4,128)(2,1)S(1)} async-done(((bf16[64,4,896]{2,1,0:T(4,128)(2,1)}), bf16[64,4,896]{2,1,0:T(4,128)(2,1)S(1)}, u32[]{:S(2)}, u32[]{:S(2)}) %all-to-all-start.2) | async-done | bytes 458784 | tf_op jit(solution)/shard_map/all_to_all | solution.py:91
  176.4 6.8 %collective-permute-start.10 = (f32[448,128]{1,0:T(8,128)S(1)}, f32[448,128]{1,0:T(8,128)S(1)}, u32[]{:S(2)}, u32[]{:S(2)}) collective-permute-start(f32[448,128]{1,0:T(8,128)S(1)} %dynamic-slice_bitcast_fusion), channel_id=1, source_target_pairs={{0,1},{1,0},{2,3},{3,2},{4,5},{5,4},{6,7},{7,6},{8,9},{9,8},{10,11... | collective-permute-start | bytes 688136 | tf_op jit(solution)/shard_map/ppermute | solution.py:19
  (75 shorter events, 22.8 us)
Async XLA Ops:
  0.0 12.1 %copy-start.9 = (s32[128,2]{0,1:T(2,128)S(1)}, s32[128,2]{0,1:T(2,128)}, u32[]{:S(2)}) copy-start(s32[128,2]{0,1:T(2,128)} %param.9) | copy-start | bytes 3076
  1.8 11.7 %all-to-all-start = ((bf16[2,2,448,128]{3,2,1,0:T(8,128)(2,1)}), bf16[2,2,448,128]{3,2,1,0:T(8,128)(2,1)S(1)}, u32[]{:S(2)}, u32[]{:S(2)}) async-start(bf16[2,2,448,128]{3,2,1,0:T(8,128)(2,1)} %pad_maximum_fusion.6), calls=%async_computation | async-start | bytes 917504 | tf_op jit(solution)/shard_map/all_to_all | solution.py:32
  13.5 1.6 copy-start.7
  15.1 1.2 copy-start.8
  19.8 34.8 %collective-permute-start = (bf16[3,896,128]{1,2,0:T(8,128)(2,1)}, bf16[3,896,128]{1,2,0:T(8,128)(2,1)S(1)}, u32[]{:S(2)}, u32[]{:S(2)}) collective-permute-start(bf16[3,896,128]{1,2,0:T(8,128)(2,1)} %get-tuple-element.22), channel_id=1, source_target_pairs={{0,2},{2,4},{4,6},{6,0},{1,3},{3,5},{5,7},{7,1},{8,10},{10,12},{12... | collective-permute-start | bytes 2064392 | tf_op jit(solution)/shard_map/ppermute | solution.py:19
  21.7 32.9 %collective-permute-start.1 = (bf16[3,896,128]{1,2,0:T(8,128)(2,1)}, bf16[3,896,128]{1,2,0:T(8,128)(2,1)S(1)}, u32[]{:S(2)}, u32[]{:S(2)}) collective-permute-start(bf16[3,896,128]{1,2,0:T(8,128)(2,1)} %get-tuple-element.21), channel_id=1, source_target_pairs={{0,4},{2,6},{4,0},{6,2},{1,5},{3,7},{5,1},{7,3},{8,12},{10,14},{12... | collective-permute-start | bytes 2064392 | tf_op jit(solution)/shard_map/ppermute | solution.py:19
  23.6 33.2 %collective-permute-start.2 = (bf16[3,896,128]{1,2,0:T(8,128)(2,1)S(1)}, bf16[3,896,128]{1,2,0:T(8,128)(2,1)S(1)}, u32[]{:S(2)}, u32[]{:S(2)}) collective-permute-start(bf16[3,896,128]{1,2,0:T(8,128)(2,1)S(1)} %get-tuple-element.20), channel_id=1, source_target_pairs={{0,6},{2,0},{4,2},{6,4},{1,7},{3,1},{5,3},{7,5},{8,14},{10,8},{12,... | collective-permute-start | bytes 2064392 | tf_op jit(solution)/shard_map/ppermute | solution.py:19
  28.2 61.2 %all-to-all-start.1 = ((bf16[64,4,1792]{2,1,0:T(4,128)(2,1)}), bf16[64,4,1792]{2,1,0:T(4,128)(2,1)}, u32[]{:S(2)}, u32[]{:S(2)}) async-start(bf16[64,4,1792]{2,1,0:T(4,128)(2,1)} %reshape.51), calls=%async_computation.1 | async-start | bytes 1835008 | tf_op jit(solution)/shard_map/all_to_all | solution.py:58
  54.6 2.7 %copy-start.3 = (bf16[3,896,128]{1,2,0:T(8,128)(2,1)}, bf16[3,896,128]{1,2,0:T(8,128)(2,1)S(1)}, u32[]{:S(2)}) copy-start(bf16[3,896,128]{1,2,0:T(8,128)(2,1)S(1)} %collective-permute-done.1) | copy-start | bytes 2064388
  57.6 8.0 %collective-permute-start.3 = (bf16[4,3,896,128]{2,3,1,0:T(8,128)(2,1)S(1)}, bf16[4,3,896,128]{2,3,1,0:T(8,128)(2,1)S(1)}, u32[]{:S(2)}, u32[]{:S(2)}) collective-permute-start(bf16[4,3,896,128]{2,3,1,0:T(8,128)(2,1)S(1)} %pad_maximum_fusion.1), channel_id=1, source_target_pairs={{0,1},{1,0},{2,3},{3,2},{4,5},{5,4},{6,7},{7,6},{8,9},{9,8},{10,11... | collective-permute-start | bytes 8257544 | tf_op jit(solution)/shard_map/ppermute | solution.py:19
  91.0 1.4 copy-start
  92.7 2.4 %copy-start.4 = (bf16[3,896,128]{1,2,0:T(8,128)(2,1)S(1)}, bf16[3,896,128]{1,2,0:T(8,128)(2,1)}, u32[]{:S(2)}) copy-start(bf16[3,896,128]{1,2,0:T(8,128)(2,1)} %copy-done.3) | copy-start | bytes 2064388
  92.7 2.4 %copy-start.6 = (bf16[3,896,128]{1,2,0:T(8,128)(2,1)S(1)}, bf16[3,896,128]{1,2,0:T(8,128)(2,1)}, u32[]{:S(2)}) copy-start(bf16[3,896,128]{1,2,0:T(8,128)(2,1)} %get-tuple-element.17) | copy-start | bytes 2064388
  93.1 11.1 %collective-permute-start.4 = (bf16[3,256,256]{2,1,0:T(8,128)(2,1)S(1)}, bf16[3,256,256]{2,1,0:T(8,128)(2,1)S(1)}, u32[]{:S(2)}, u32[]{:S(2)}) collective-permute-start(bf16[3,256,256]{2,1,0:T(8,128)(2,1)S(1)} %pad_maximum_fusion.7), channel_id=1, source_target_pairs={{0,6},{2,0},{4,2},{6,4},{1,7},{3,1},{5,3},{7,5},{8,14},{10,8},{12,... | collective-permute-start | bytes 1179656 | tf_op jit(solution)/shard_map/ppermute | solution.py:19
  95.8 4.5 %copy-start.2 = (bf16[3,896,128]{1,2,0:T(8,128)(2,1)S(1)}, bf16[3,896,128]{1,2,0:T(8,128)(2,1)}, u32[]{:S(2)}) copy-start(bf16[3,896,128]{1,2,0:T(8,128)(2,1)} %copy-done.1) | copy-start | bytes 2064388
  95.8 4.5 %copy-start.5 = (bf16[3,896,128]{1,2,0:T(8,128)(2,1)S(1)}, bf16[3,896,128]{1,2,0:T(8,128)(2,1)}, u32[]{:S(2)}) copy-start(bf16[3,896,128]{1,2,0:T(8,128)(2,1)} %get-tuple-element.16) | copy-start | bytes 2064388
  96.2 10.0 %collective-permute-start.5 = (bf16[3,256,256]{2,1,0:T(8,128)(2,1)S(1)}, bf16[3,256,256]{2,1,0:T(8,128)(2,1)S(1)}, u32[]{:S(2)}, u32[]{:S(2)}) collective-permute-start(bf16[3,256,256]{2,1,0:T(8,128)(2,1)S(1)} %pad_maximum_fusion.8), channel_id=1, source_target_pairs={{0,4},{2,6},{4,0},{6,2},{1,5},{3,7},{5,1},{7,3},{8,12},{10,14},{12... | collective-permute-start | bytes 1179656 | tf_op jit(solution)/shard_map/ppermute | solution.py:19
  101.3 15.2 %collective-permute-start.6 = (bf16[3,256,256]{2,1,0:T(8,128)(2,1)S(1)}, bf16[3,256,256]{2,1,0:T(8,128)(2,1)S(1)}, u32[]{:S(2)}, u32[]{:S(2)}) collective-permute-start(bf16[3,256,256]{2,1,0:T(8,128)(2,1)S(1)} %pad_maximum_fusion.9), channel_id=1, source_target_pairs={{0,2},{2,4},{4,6},{6,0},{1,3},{3,5},{5,7},{7,1},{8,10},{10,12},{12... | collective-permute-start | bytes 1179656 | tf_op jit(solution)/shard_map/ppermute | solution.py:19
  117.2 15.7 %collective-permute-start.7 = (bf16[2,256,256]{2,1,0:T(8,128)(2,1)S(1)}, bf16[2,256,256]{2,1,0:T(8,128)(2,1)S(1)}, u32[]{:S(2)}, u32[]{:S(2)}) collective-permute-start(bf16[2,256,256]{2,1,0:T(8,128)(2,1)S(1)} %pad_maximum_fusion.10), channel_id=1, source_target_pairs={{0,2},{2,4},{4,6},{6,0},{1,3},{3,5},{5,7},{7,1},{8,10},{10,12},{12... | collective-permute-start | bytes 786440 | tf_op jit(solution)/shard_map/ppermute | solution.py:19
  119.1 10.6 %collective-permute-start.8 = (bf16[2,256,256]{2,1,0:T(8,128)(2,1)S(1)}, bf16[2,256,256]{2,1,0:T(8,128)(2,1)S(1)}, u32[]{:S(2)}, u32[]{:S(2)}) collective-permute-start(bf16[2,256,256]{2,1,0:T(8,128)(2,1)S(1)} %pad_maximum_fusion.10), channel_id=1, source_target_pairs={{0,4},{2,6},{4,0},{6,2},{1,5},{3,7},{5,1},{7,3},{8,12},{10,14},{12... | collective-permute-start | bytes 786440 | tf_op jit(solution)/shard_map/ppermute | solution.py:19
  123.1 9.2 %collective-permute-start.9 = (bf16[2,256,256]{2,1,0:T(8,128)(2,1)S(1)}, bf16[2,256,256]{2,1,0:T(8,128)(2,1)S(1)}, u32[]{:S(2)}, u32[]{:S(2)}) collective-permute-start(bf16[2,256,256]{2,1,0:T(8,128)(2,1)S(1)} %pad_maximum_fusion.10), channel_id=1, source_target_pairs={{0,6},{2,0},{4,2},{6,4},{1,7},{3,1},{5,3},{7,5},{8,14},{10,8},{12,... | collective-permute-start | bytes 786440 | tf_op jit(solution)/shard_map/ppermute | solution.py:19
  133.7 15.8 %copy-start.10 = (f32[128,2]{0,1:T(2,128)S(1)}, f32[128,2]{0,1:T(2,128)}, u32[]{:S(2)}) copy-start(f32[128,2]{0,1:T(2,128)} %param.10) | copy-start | bytes 3076
  134.6 41.3 %all-to-all-start.2 = ((bf16[64,4,896]{2,1,0:T(4,128)(2,1)}), bf16[64,4,896]{2,1,0:T(4,128)(2,1)S(1)}, u32[]{:S(2)}, u32[]{:S(2)}) async-start(bf16[64,4,896]{2,1,0:T(4,128)(2,1)} %reshape.53), calls=%async_computation.2 | async-start | bytes 917504 | tf_op jit(solution)/shard_map/all_to_all | solution.py:91
  176.4 7.9 %collective-permute-start.10 = (f32[448,128]{1,0:T(8,128)S(1)}, f32[448,128]{1,0:T(8,128)S(1)}, u32[]{:S(2)}, u32[]{:S(2)}) collective-permute-start(f32[448,128]{1,0:T(8,128)S(1)} %dynamic-slice_bitcast_fusion), channel_id=1, source_target_pairs={{0,1},{1,0},{2,3},{3,2},{4,5},{5,4},{6,7},{7,6},{8,9},{9,8},{10,11... | collective-permute-start | bytes 688136 | tf_op jit(solution)/shard_map/ppermute | solution.py:19
  (1 other events, 0.9 us)
